TPU v7x, 32 devices: a whole 2x2x4 slice. The times are simulated.
32 devices in a mesh: run: 2 (over y), tile: 8 (over z, x), depth: 2 (over core).
Axes of the slice: x: 2, y: 2, z: 4, core: 2. Of those that a mesh axis runs over, the one named last changes fastest.
Arguments:
- dissolved: bfloat16 [128, 16, 256], P(('run', 'tile', 'depth')), parts along dimension 0, may hold values from -6 to 6
- sorbed: bfloat16 [128, 16, 256], P(('run', 'tile', 'depth')), parts along dimension 0, may hold values from -6 to 6
- tf_table: float32 [4, 256], replicated, may hold values from 0.1 to 1
Outputs:
- gradient_norms: float32 [2, 128, 16, 256], P(None, ('run', 'tile', 'depth')), parts along dimension 1
- rendered: float32 [4, 32, 256], P(None, ('run', 'tile', 'depth')), parts along dimension 1
There are 2 independent parts, one for each index of `run`. A program takes and returns all parts, laid end to end along the dimension named above; an argument that names none is the same for every part. Nothing has to cross between parts.
All inputs are finite; a program needn't handle non-finite values.
Results may differ from a plain program's by a relative error of at most 0.0003.
Values may be sent and summed in bfloat16 or wider, within the bound.
A program may use at most 320 MiB of HBM per device.

v0:
```python
from functools import partial
import math

import jax
import jax.numpy as jnp
from jax import lax
from jax.sharding import PartitionSpec as P

spread_cells = 1.5
cell_spacing = 0.05
bell_values = [
    math.exp(-(offset * offset) / (2.0 * spread_cells * spread_cells)) for offset in range(-3, 4)
]
gauss_taps = [value / sum(bell_values) for value in bell_values]
slope_norm = sum(((offset - 3) * (offset - 3) * bell_values[offset] for offset in range(7)))
slope_taps = [(offset - 3) * bell_values[offset] / slope_norm / cell_spacing for offset in range(7)]
light_vector = (0.48, 0.6, 0.64)


def swapped(block, axis, bit):
    count = lax.axis_size(axis)
    route = []
    for low in range(count):
        high = low | 1 << bit
        if high != low and high < count:
            route += [(low, high), (high, low)]
    return lax.ppermute(block, axis, route)


def extended(cells, sides, width):
    for axis, dim in sides:
        count = lax.axis_size(axis)
        ends = count - 1
        head = lax.slice_in_dim(cells, 0, width, axis=dim)
        tail = lax.slice_in_dim(cells, cells.shape[dim] - width, cells.shape[dim], axis=dim)
        cells = jnp.concatenate(
            [
                lax.ppermute(tail, axis, [(i, (i + 1) % count) for i in range(ends)]),
                cells,
                lax.ppermute(head, axis, [((i + 1) % count, i) for i in range(ends)]),
            ],
            axis=dim,
        )
    return cells


def apply_taps(source, along_dim, weights, length):
    summed = weights[0] * lax.slice_in_dim(source, 0, length, axis=along_dim)
    for offset in range(1, 7):
        summed = summed + weights[offset] * lax.slice_in_dim(
            source, offset, offset + length, axis=along_dim
        )
    return summed


def band_matrix(length, weights):
    row_ids = lax.broadcasted_iota(jnp.int32, (length, length), 0)
    col_ids = lax.broadcasted_iota(jnp.int32, (length, length), 1)
    offsets = col_ids - row_ids
    matrix = jnp.zeros((length, length), jnp.float32)
    for offset in range(7):
        matrix = matrix + jnp.where(offsets == offset - 3, weights[offset], 0.0)
    return matrix


def filter_rows(source, matrix):
    return jnp.einsum("fzxy,wx->fzwy", source, matrix, precision=lax.Precision.HIGHEST)


def filter_columns(source, matrix):
    return jnp.einsum("fzxy,wy->fzxw", source, matrix, precision=lax.Precision.HIGHEST)


def shade_cells(window, table, z_first, total_depth):
    depth_cells = window.shape[1] - 6
    fields = window.astype(jnp.float32)
    rows = fields.shape[2]
    columns = fields.shape[3]
    gauss_rows = band_matrix(rows, gauss_taps)
    slope_rows = band_matrix(rows, slope_taps)
    gauss_cols = band_matrix(columns, gauss_taps)
    slope_cols = band_matrix(columns, slope_taps)
    smooth_z = apply_taps(fields, 1, gauss_taps, depth_cells)
    slope_z = apply_taps(fields, 1, slope_taps, depth_cells)
    smooth_zx = filter_rows(smooth_z, gauss_rows)
    grad_x = filter_columns(filter_rows(smooth_z, slope_rows), gauss_cols)
    grad_y = filter_columns(smooth_zx, slope_cols)
    grad_z = filter_columns(filter_rows(slope_z, gauss_rows), gauss_cols)
    squared = grad_x * grad_x + grad_y * grad_y + grad_z * grad_z
    grad_norms = jnp.sqrt(squared)
    concentration = fields[0, 3 : 3 + depth_cells]
    entries = table.shape[1]
    position = jax.nn.sigmoid(concentration) * (entries - 1)
    lower_idx = jnp.minimum(jnp.floor(position), entries - 2)
    weight_hi = position - lower_idx
    index_low = lower_idx.astype(jnp.int32)
    lower_entry = jnp.take(table, index_low, axis=1)
    upper_entry = jnp.take(table, index_low + 1, axis=1)
    looked = lower_entry + weight_hi[None] * (upper_entry - lower_entry)
    facing = light_vector[0] * grad_z[0] + light_vector[1] * grad_x[0] + light_vector[2] * grad_y[0]
    shading = 0.25 + 0.75 * jnp.abs(facing) / jnp.sqrt(1.0 + squared[0])
    heights = (z_first + jnp.arange(depth_cells, dtype=jnp.int32)).astype(jnp.float32)
    depth_cue = 1.0 - 0.5 * (heights + 0.5) / total_depth
    sorb_term = squared[1] / (1.0 + squared[1])
    extinct = 3.0 / total_depth * looked[3] * (1.0 + sorb_term)
    opacity = -jnp.expm1(-extinct)
    colors = looked[:3] * (shading * depth_cue[:, None, None] * opacity)[None]
    return (grad_norms, colors, extinct)


def compose_over(front_part, back_part):
    emitted = front_part[:3] + front_part[3:] * back_part[:3]
    transmit = front_part[3:] * back_part[3:]
    return jnp.concatenate([emitted, transmit], axis=0)


def swap_round(partial_image, own_bit, partner_fn):
    blocks = partial_image.shape[1]
    paired = partial_image.reshape((4, blocks // 2, 2) + partial_image.shape[2:])
    lower_half = paired[:, :, 0]
    upper_half = paired[:, :, 1]
    in_front = own_bit == 0
    kept_half = jnp.where(in_front, lower_half, upper_half)
    sent_half = jnp.where(in_front, upper_half, lower_half)
    received = partner_fn(sent_half)
    front_part = jnp.where(in_front, kept_half, received)
    back_part = jnp.where(in_front, received, kept_half)
    return compose_over(front_part, back_part)


def depth_partner(piece):
    return swapped(piece, "depth", 0)


def tile_partner(piece, level):
    return swapped(piece, "tile", level)


def local(dissolved, sorbed, tf_table):
    bricks = jnp.stack([dissolved, sorbed])
    padded = extended(bricks, ((("tile", "depth"), 1),), 3)
    depth_cells = dissolved.shape[0]
    tile_count = lax.axis_size("tile")
    depth_count = lax.axis_size("depth")
    slab_index = lax.axis_index("tile") * depth_count + lax.axis_index("depth")
    total_depth = depth_cells * tile_count * depth_count
    grad_norms, colors, extinct = shade_cells(
        padded, tf_table, slab_index * depth_cells, total_depth
    )
    prefix = jnp.cumsum(extinct, axis=0) - extinct
    emitted = jnp.sum(colors * jnp.exp(-prefix)[None], axis=1)
    transmit = jnp.exp(-jnp.sum(extinct, axis=0))
    picture = jnp.concatenate([emitted, transmit[None]], axis=0)
    blocks = tile_count * depth_count
    rows = picture.shape[1] // blocks
    columns = picture.shape[2]
    partial_image = picture.reshape(4, blocks, rows, columns)
    partial_image = swap_round(partial_image, lax.axis_index("depth"), depth_partner)
    levels = tile_count.bit_length() - 1
    tile_position = lax.axis_index("tile")
    for level in range(levels):
        own_bit = jnp.right_shift(tile_position, level) & 1
        partial_image = swap_round(partial_image, own_bit, partial(tile_partner, level=level))
    finished = partial_image.reshape(4, rows, columns)
    rendered = jnp.concatenate([finished[:3], 1.0 - finished[3:]], axis=0)
    return (grad_norms, rendered)


def solution(mesh):
    return jax.shard_map(
        local,
        mesh=mesh,
        in_specs=(
            P(("run", "tile", "depth"), None, None),
            P(("run", "tile", "depth"), None, None),
            P(),
        ),
        out_specs=(
            P(None, ("run", "tile", "depth"), None, None),
            P(None, ("run", "tile", "depth"), None),
        ),
        check_vma=False,
    )
```

profile of v0, /device:TPU:0, one launch (start us, length us, event | category | flops | bytes accessed | tf_op | source)
XLA Modules:
  0.0 150.3 jit_solution(12623603582307245115)
XLA Ops:
  0.6 0.8 fusion.99
  1.5 2.4 %collective-permute-start = (bf16[2,3,16,256]{3,2,1,0:T(8,128)(2,1)S(1)}, bf16[2,3,16,256]{3,2,1,0:T(8,128)(2,1)S(1)}, u32[]{:S(2)}, u32[]{:S(2)}) collective-permute-start(bf16[2,3,16,256]{3,2,1,0:T(8,128)(2,1)S(1)} %get-tuple-element.13), channel_id=1, source_target_pairs={{0,1},{1,2},{2,3},{3,4},{4,5},{5,6},{6,7},{7,8},{8,9},{9,10},{10,1... | collective-permute-start | bytes 147464 | tf_op jit(solution)/shard_map/ppermute | solution.py:38
  3.8 1.3 collective-permute-start.1
  5.2 0.8 copy.19
  6.0 3.1 %collective-permute-done.1 = bf16[2,3,16,256]{3,2,1,0:T(8,128)(2,1)S(1)} collective-permute-done((bf16[2,3,16,256]{3,2,1,0:T(8,128)(2,1)S(1)}, bf16[2,3,16,256]{3,2,1,0:T(8,128)(2,1)S(1)}, u32[]{:S(2)}, u32[]{:S(2)}) %collective-permute-start.1) | collective-permute-done | bytes 49184 | tf_op jit(solution)/shard_map/ppermute | solution.py:40
  9.1 0.8 maximum_convert_fusion
  10.4 0.3 convolution_bitcast_fusion.2
  10.6 0.3 convolution_bitcast_fusion
  11.0 54.4 %gather_fusion = f32[16384,4]{1,0:T(8,128)} fusion(f32[4,256]{0,1:T(8,128)S(1)} %copy.19, s32[16384]{0:T(1024)S(1)} %broadcast_clamp_fusion.1), kind=kCustom, calls=%fused_computation.clone | custom fusion | bytes 589824 | tf_op jit(solution)/shard_map/jit(_take)/gather | solution.py:97
  65.4 5.2 %copy.39 = f32[4,16,256,4]{2,1,0,3:T(8,128)S(1)} copy(f32[4,16,256,4]{3,2,1,0:T(8,128)} %bitcast.161) | data formatting | bytes 524288 | tf_op jit(solution)/shard_map/jit(_take)/gather | solution.py:97
  70.7 54.4 %gather_fusion.1 = f32[16384,4]{1,0:T(8,128)} fusion(f32[4,256]{0,1:T(8,128)S(1)} %copy.19, s32[16384]{0:T(1024)S(1)} %broadcast_clamp_fusion), kind=kCustom, calls=%fused_computation.1.clone | custom fusion | bytes 589824 | tf_op jit(solution)/shard_map/jit(_take)/gather | solution.py:98
  125.2 5.2 %copy.40 = f32[4,16,256,4]{2,1,0,3:T(8,128)S(1)} copy(f32[4,16,256,4]{3,2,1,0:T(8,128)} %bitcast.160) | data formatting | bytes 524288 | tf_op jit(solution)/shard_map/jit(_take)/gather | solution.py:98
  130.4 0.4 fusion.3
  130.9 0.5 fusion.9
  131.3 1.1 fusion.237
  133.0 2.8 %collective-permute-start.2 = (f32[4,8,1,256]{3,2,1,0:T(1,128)S(1)}, f32[4,8,1,256]{3,2,1,0:T(1,128)S(1)}, u32[]{:S(2)}, u32[]{:S(2)}) collective-permute-start(f32[4,8,1,256]{3,2,1,0:T(1,128)S(1)} %get-tuple-element.3), channel_id=1, source_target_pairs={{0,1},{1,0},{2,3},{3,2},{4,5},{5,4},{6,7},{7,6},{8,9},{9,8},{10,11... | collective-permute-start | bytes 98312 | tf_op jit(solution)/shard_map/ppermute | solution.py:27
  135.8 0.9 collective-permute-done.2
  136.9 2.5 %collective-permute-start.3 = (f32[4,4,1,256]{3,0,1,2:T(4,128)S(1)}, f32[4,4,1,256]{3,0,1,2:T(4,128)S(1)}, u32[]{:S(2)}, u32[]{:S(2)}) collective-permute-start(f32[4,4,1,256]{3,0,1,2:T(4,128)S(1)} %select_bitcast_fusion), channel_id=1, source_target_pairs={{0,2},{2,0},{4,6},{6,4},{8,10},{10,8},{12,14},{14,12},{1,3},{3,1},... | collective-permute-start | bytes 49160 | tf_op jit(solution)/shard_map/ppermute | solution.py:27
  139.4 1.7 %collective-permute-done.3 = f32[4,4,1,256]{3,0,1,2:T(4,128)S(1)} collective-permute-done((f32[4,4,1,256]{3,0,1,2:T(4,128)S(1)}, f32[4,4,1,256]{3,0,1,2:T(4,128)S(1)}, u32[]{:S(2)}, u32[]{:S(2)}) %collective-permute-start.3) | collective-permute-done | bytes 16416 | tf_op jit(solution)/shard_map/ppermute | solution.py:27
  141.2 1.6 %collective-permute-start.4 = (f32[4,2,1,256]{3,2,1,0:T(1,128)S(1)}, f32[4,2,1,256]{3,2,1,0:T(1,128)S(1)}, u32[]{:S(2)}, u32[]{:S(2)}) collective-permute-start(f32[4,2,1,256]{3,2,1,0:T(1,128)S(1)} %fusion.107), channel_id=1, source_target_pairs={{0,4},{4,0},{2,6},{6,2},{8,12},{12,8},{10,14},{14,10},{1,5},{5,1},... | collective-permute-start | bytes 24584 | tf_op jit(solution)/shard_map/ppermute | solution.py:27
  142.9 2.1 %collective-permute-done.4 = f32[4,2,1,256]{3,2,1,0:T(1,128)S(1)} collective-permute-done((f32[4,2,1,256]{3,2,1,0:T(1,128)S(1)}, f32[4,2,1,256]{3,2,1,0:T(1,128)S(1)}, u32[]{:S(2)}, u32[]{:S(2)}) %collective-permute-start.4) | collective-permute-done | bytes 8224 | tf_op jit(solution)/shard_map/ppermute | solution.py:27
  145.0 2.7 %collective-permute-start.5 = (f32[4,1,1,256]{3,1,2,0:T(1,128)S(1)}, f32[4,1,1,256]{3,1,2,0:T(1,128)S(1)}, u32[]{:S(2)}, u32[]{:S(2)}) collective-permute-start(f32[4,1,1,256]{3,1,2,0:T(1,128)S(1)} %fusion.137), channel_id=1, source_target_pairs={{0,8},{8,0},{2,10},{10,2},{4,12},{12,4},{6,14},{14,6},{1,9},{9,1},... | collective-permute-start | bytes 12296 | tf_op jit(solution)/shard_map/ppermute | solution.py:27
  147.7 1.9 %collective-permute-done.5 = f32[4,1,1,256]{3,1,2,0:T(1,128)S(1)} collective-permute-done((f32[4,1,1,256]{3,1,2,0:T(1,128)S(1)}, f32[4,1,1,256]{3,1,2,0:T(1,128)S(1)}, u32[]{:S(2)}, u32[]{:S(2)}) %collective-permute-start.5) | collective-permute-done | bytes 4128 | tf_op jit(solution)/shard_map/ppermute | solution.py:27
  149.7 0.6 pad_maximum_fusion.4
  (44 shorter events, 1.3 us)
Async XLA Ops:
  1.5 4.5 %collective-permute-start = (bf16[2,3,16,256]{3,2,1,0:T(8,128)(2,1)S(1)}, bf16[2,3,16,256]{3,2,1,0:T(8,128)(2,1)S(1)}, u32[]{:S(2)}, u32[]{:S(2)}) collective-permute-start(bf16[2,3,16,256]{3,2,1,0:T(8,128)(2,1)S(1)} %get-tuple-element.13), channel_id=1, source_target_pairs={{0,1},{1,2},{2,3},{3,4},{4,5},{5,6},{6,7},{7,8},{8,9},{9,10},{10,1... | collective-permute-start | bytes 147464 | tf_op jit(solution)/shard_map/ppermute | solution.py:38
  3.8 5.2 %collective-permute-start.1 = (bf16[2,3,16,256]{3,2,1,0:T(8,128)(2,1)S(1)}, bf16[2,3,16,256]{3,2,1,0:T(8,128)(2,1)S(1)}, u32[]{:S(2)}, u32[]{:S(2)}) collective-permute-start(bf16[2,3,16,256]{3,2,1,0:T(8,128)(2,1)S(1)} %get-tuple-element.14), channel_id=1, source_target_pairs={{1,0},{2,1},{3,2},{4,3},{5,4},{6,5},{7,6},{8,7},{9,8},{10,9},{11,1... | collective-permute-start | bytes 147464 | tf_op jit(solution)/shard_map/ppermute | solution.py:40
  133.0 3.7 %collective-permute-start.2 = (f32[4,8,1,256]{3,2,1,0:T(1,128)S(1)}, f32[4,8,1,256]{3,2,1,0:T(1,128)S(1)}, u32[]{:S(2)}, u32[]{:S(2)}) collective-permute-start(f32[4,8,1,256]{3,2,1,0:T(1,128)S(1)} %get-tuple-element.3), channel_id=1, source_target_pairs={{0,1},{1,0},{2,3},{3,2},{4,5},{5,4},{6,7},{7,6},{8,9},{9,8},{10,11... | collective-permute-start | bytes 98312 | tf_op jit(solution)/shard_map/ppermute | solution.py:27
  136.9 4.2 %collective-permute-start.3 = (f32[4,4,1,256]{3,0,1,2:T(4,128)S(1)}, f32[4,4,1,256]{3,0,1,2:T(4,128)S(1)}, u32[]{:S(2)}, u32[]{:S(2)}) collective-permute-start(f32[4,4,1,256]{3,0,1,2:T(4,128)S(1)} %select_bitcast_fusion), channel_id=1, source_target_pairs={{0,2},{2,0},{4,6},{6,4},{8,10},{10,8},{12,14},{14,12},{1,3},{3,1},... | collective-permute-start | bytes 49160 | tf_op jit(solution)/shard_map/ppermute | solution.py:27
  141.2 3.7 %collective-permute-start.4 = (f32[4,2,1,256]{3,2,1,0:T(1,128)S(1)}, f32[4,2,1,256]{3,2,1,0:T(1,128)S(1)}, u32[]{:S(2)}, u32[]{:S(2)}) collective-permute-start(f32[4,2,1,256]{3,2,1,0:T(1,128)S(1)} %fusion.107), channel_id=1, source_target_pairs={{0,4},{4,0},{2,6},{6,2},{8,12},{12,8},{10,14},{14,10},{1,5},{5,1},... | collective-permute-start | bytes 24584 | tf_op jit(solution)/shard_map/ppermute | solution.py:27
  145.0 4.6 %collective-permute-start.5 = (f32[4,1,1,256]{3,1,2,0:T(1,128)S(1)}, f32[4,1,1,256]{3,1,2,0:T(1,128)S(1)}, u32[]{:S(2)}, u32[]{:S(2)}) collective-permute-start(f32[4,1,1,256]{3,1,2,0:T(1,128)S(1)} %fusion.137), channel_id=1, source_target_pairs={{0,8},{8,0},{2,10},{10,2},{4,12},{12,4},{6,14},{14,6},{1,9},{9,1},... | collective-permute-start | bytes 12296 | tf_op jit(solution)/shard_map/ppermute | solution.py:27
where the time goes:
time: 151 us; the launch traced here: 150 us
  local copies, waits for them, and re-layouts  120 us (79%)
  starting transfers between devices  13.3 us (9%)
  waiting for transfers between devices  9.63 us (6%)
  other arithmetic  3.18 us (2%)
  matrix products  2.85 us (2%)
    gather x2, local copies, waits for them, and re-layouts, shade_cells(): lower_entry = jnp.take(table, index_low, axis=1)  59.7 us
    gather x2, local copies, waits for them, and re-layouts, shade_cells(): upper_entry = jnp.take(table, index_low + 1, axis=1)  59.7 us
    ppermute x4, starting transfers between devices, swapped(): return lax.ppermute(block, axis, route)  9.65 us
    ppermute x4, waiting for transfers between devices, swapped(): return lax.ppermute(block, axis, route)  6.56 us
    ppermute x1, waiting for transfers between devices, extended(): lax.ppermute(head, axis, [((i + 1) % count, i) for i in range(ends)])  3.07 us
  transfers between devices with their start and end apart: 6, of which 5 were waited for; matrix products, arithmetic and copies ran while one was open for 1% of the time, Pallas kernels for 0%

commit v1 on v0

v1 whole, which is shorter than its diff:
```python
import functools
import math

import jax
import jax.numpy as jnp
from jax import lax
from jax.experimental import pallas as pl
from jax.experimental.pallas import tpu as pltpu
from jax.sharding import PartitionSpec as P

MESH = pl.DeviceIdType.MESH
REACH = 3
SPREAD = 4.5
ROWS = 16
LANES = 128
BELL = [math.exp(-(k * k) / SPREAD) for k in range(-REACH, REACH + 1)]
SMOOTH = 1.0 / sum(BELL)
SLOPE = 20.0 / sum(k * k * BELL[k + REACH] for k in range(-REACH, REACH + 1))
LIGHT = (0.48, 0.6, 0.64)


def two_parts(values):
    high = values.astype(jnp.bfloat16)
    low = (values - high.astype(jnp.float32)).astype(jnp.bfloat16)
    return high, low


def plane_weights(weights_ref, depth, window, shift):
    cells = depth * ROWS
    shape = (cells, (depth + 2 * REACH) * window)
    row = lax.broadcasted_iota(jnp.int32, shape, 0)
    col = lax.broadcasted_iota(jnp.int32, shape, 1)
    dz = col // window - row // ROWS - REACH
    dx = col % window - row % ROWS - shift
    near = (jnp.abs(dz) <= REACH) & (jnp.abs(dx) <= REACH)
    dz = dz.astype(jnp.float32)
    dx = dx.astype(jnp.float32)
    bell = jnp.where(near, jnp.exp((dz * dz + dx * dx) * (-1.0 / SPREAD)), 0.0)
    parts = (
        bell * dz * (SLOPE * SMOOTH),
        bell * dx * (SLOPE * SMOOTH),
        bell * (SMOOTH * SMOOTH),
    )
    for k, part in enumerate(parts):
        high, low = two_parts(part)
        weights_ref[pl.ds(k * cells, cells), :] = high
        weights_ref[pl.ds((k + 3) * cells, cells), :] = low


def line_weights(lines_ref, columns):
    shape = (columns, columns)
    offset = lax.broadcasted_iota(jnp.int32, shape, 0) - lax.broadcasted_iota(jnp.int32, shape, 1)
    near = jnp.abs(offset) <= REACH
    offset = offset.astype(jnp.float32)
    bell = jnp.where(near, jnp.exp(offset * offset * (-1.0 / SPREAD)), 0.0)
    lines_ref[0], lines_ref[1] = two_parts(bell * SMOOTH)
    lines_ref[2], lines_ref[3] = two_parts(bell * offset * SLOPE)


def matmul(a, b):
    return jnp.dot(a, b, preferred_element_type=jnp.float32)


def lookup(table, step, position):
    lower = jnp.minimum(jnp.floor(position), table.shape[1] - 2.0)
    fraction = position - lower
    index = lower.astype(jnp.int32)
    lane = index % LANES
    group = index // LANES
    values = []
    for c in range(4):
        base = None
        for g in range(table.shape[1] // LANES):
            pair = []
            for source in (table, step):
                entries = jnp.broadcast_to(
                    source[c : c + 1, g * LANES : (g + 1) * LANES], position.shape
                )
                pair.append(
                    jnp.take_along_axis(entries, lane, axis=1, mode="promise_in_bounds")
                )
            if base is None:
                base, slope = pair
            else:
                base = jnp.where(group == g, pair[0], base)
                slope = jnp.where(group == g, pair[1], slope)
        values.append(base + fraction * slope)
    return values


def kernel(
    tiles, depths, dissolved, sorbed, table_ref, norms, rendered,
    cells, weights, lines, looked, send, recv,
    halo_send, halo_recv, image_send, image_recv,
):
    depth, rows, columns = dissolved.shape
    group = tiles * depths
    total = depth * group
    chunks = rows // ROWS
    shift = 0 if chunks == 1 else ROWS
    window = ROWS + 2 * shift
    halves = columns // LANES
    run = lax.axis_index("run")
    me = lax.axis_index("tile") * depths + lax.axis_index("depth")

    def device(slab):
        return (run, slab // depths, slab % depths)

    def peers(body):
        if group <= 32:
            for k in range(1, group):
                body(lax.rem(me + k, group))
        else:
            @pl.loop(1, group)
            def _(k):
                body(lax.rem(me + k, group))

    barrier = pltpu.get_barrier_semaphore()
    peers(lambda p: pl.semaphore_signal(barrier, inc=1, device_id=device(p), device_id_type=MESH))
    pl.semaphore_wait(barrier, group - 1)

    inner = pl.ds(shift, rows)

    def halo(field, up):
        source = (dissolved, sorbed)[field]
        k = 2 * field + up
        return pltpu.make_async_remote_copy(
            src_ref=source.at[pl.ds(depth - REACH, REACH)] if up else source.at[pl.ds(0, REACH)],
            dst_ref=cells.at[field, pl.ds(0 if up else depth + REACH, REACH), inner],
            send_sem=halo_send.at[k],
            recv_sem=halo_recv.at[k],
            device_id=device(me + 1 if up else me - 1),
            device_id_type=MESH,
        )

    first, last = me == 0, me == group - 1

    @pl.when(jnp.logical_not(last))
    def _():
        for field in range(2):
            halo(field, 1).start()

    @pl.when(jnp.logical_not(first))
    def _():
        for field in range(2):
            halo(field, 0).start()

    @pl.when(first)
    def _():
        for field in range(2):
            cells[field, pl.ds(0, REACH), inner] = jnp.zeros((REACH, rows, columns), jnp.bfloat16)

    @pl.when(last)
    def _():
        for field in range(2):
            cells[field, pl.ds(depth + REACH, REACH), inner] = jnp.zeros(
                (REACH, rows, columns), jnp.bfloat16
            )

    if shift:
        edge = jnp.zeros((depth + 2 * REACH, shift, columns), jnp.bfloat16)
        for field in range(2):
            cells[field, :, pl.ds(0, shift)] = edge
            cells[field, :, pl.ds(shift + rows, shift)] = edge
    cells[0, pl.ds(REACH, depth), inner] = dissolved[...]
    cells[1, pl.ds(REACH, depth), inner] = sorbed[...]

    plane_weights(weights, depth, window, shift)
    line_weights(lines, columns)

    table = table_ref[...]
    step = pltpu.roll(table, table.shape[1] - 1, 1) - table

    def look(x0):
        for z in range(depth):
            level = dissolved[z, pl.ds(x0, ROWS), :].astype(jnp.float32)
            position = (table.shape[1] - 1.0) / (1.0 + jnp.exp(-level))
            for h in range(halves):
                span = slice(h * LANES, (h + 1) * LANES)
                for r in range(0, ROWS, 8):
                    found = lookup(table, step, position[r : r + 8, span])
                    for c in range(4):
                        looked[c, z, pl.ds(r, 8), span] = found[c]

    def shade(x0):
        plane = depth * ROWS
        flat = []
        for field in range(2):
            piece = cells[field, :, pl.ds(x0, window), :].reshape(-1, columns)
            both = matmul(weights[...], piece)
            flat.append(both[: 3 * plane] + both[3 * plane :])
        smooth_in = jnp.concatenate([flat[0][: 2 * plane], flat[1][: 2 * plane]], axis=0)
        slope_in = jnp.concatenate([flat[0][2 * plane :], flat[1][2 * plane :]], axis=0)
        high, low = two_parts(smooth_in)
        smoothed = matmul(high, lines[0]) + matmul(low, lines[0]) + matmul(high, lines[1])
        high, low = two_parts(slope_in)
        sloped = matmul(high, lines[2]) + matmul(low, lines[2]) + matmul(high, lines[3])

        emitted = [None] * 3
        transmit = None
        for z in range(depth):
            here = slice(z * ROWS, (z + 1) * ROWS)
            squares = []
            for field in range(2):
                gz = smoothed[2 * field * plane :][here]
                gx = smoothed[(2 * field + 1) * plane :][here]
                gy = sloped[field * plane :][here]
                square = gx * gx + gy * gy + gz * gz
                norms[field, z, pl.ds(x0, ROWS), :] = jnp.sqrt(square)
                squares.append(square)
                if field == 0:
                    facing = LIGHT[0] * gz + LIGHT[1] * gx + LIGHT[2] * gy
            shading = 0.25 + 0.75 * jnp.abs(facing) * lax.rsqrt(1.0 + squares[0])
            height = (me * depth + z).astype(jnp.float32)
            cue = 1.0 - (height + 0.5) * (0.5 / total)
            extinct = (3.0 / total) * looked[3, z] * (2.0 - 1.0 / (1.0 + squares[1]))
            passing = jnp.exp(-extinct)
            strength = shading * cue * (1.0 - passing)
            if z:
                strength = strength * transmit
            for c in range(3):
                colour = looked[c, z] * strength
                emitted[c] = colour if z == 0 else emitted[c] + colour
            transmit = passing if z == 0 else transmit * passing
        for c, layer in enumerate(emitted + [transmit]):
            for h in range(halves):
                send[pl.ds(x0, ROWS), c * halves + h, :] = layer[:, h * LANES : (h + 1) * LANES]

    def arrive():
        @pl.when(jnp.logical_not(first))
        def _():
            for field in range(2):
                halo(field, 1).wait_recv()

        @pl.when(jnp.logical_not(last))
        def _():
            for field in range(2):
                halo(field, 0).wait_recv()

    if chunks == 1:
        look(0)
        arrive()
        shade(0)
    else:
        arrive()

        @pl.loop(0, chunks)
        def _(chunk):
            x0 = pl.multiple_of(chunk * ROWS, ROWS)
            look(x0)
            shade(x0)

    def image(slab):
        return pltpu.make_async_remote_copy(
            src_ref=send.at[slab],
            dst_ref=recv.at[me],
            send_sem=image_send,
            recv_sem=image_recv,
            device_id=device(slab),
            device_id_type=MESH,
        )

    peers(lambda p: image(p).start())
    recv[me] = send[me]

    others = pltpu.make_async_remote_copy(
        src_ref=send.at[pl.ds(0, group - 1)],
        dst_ref=recv.at[pl.ds(0, group - 1)],
        send_sem=image_send,
        recv_sem=image_recv,
        device_id=device(lax.rem(me + 1, group)),
        device_id_type=MESH,
    )
    others.wait_recv()

    order = lax.broadcasted_iota(jnp.int32, (group, LANES), 0)
    for h in range(halves):
        span = slice(h * LANES, (h + 1) * LANES)
        through = recv[:, 3 * halves + h, :]
        hop = 1
        while hop < group:
            through = through * jnp.where(order >= hop, pltpu.roll(through, hop, 0), 1.0)
            hop *= 2
        ahead = jnp.where(order >= 1, pltpu.roll(through, 1, 0), 1.0)
        for c in range(3):
            rendered[c, :, span] = jnp.sum(
                recv[:, c * halves + h, :] * ahead, axis=0, keepdims=True
            )
        rendered[3, :, span] = 1.0 - through[group - 1 :]

    @pl.when(jnp.logical_not(last))
    def _():
        for field in range(2):
            halo(field, 1).wait_send()

    @pl.when(jnp.logical_not(first))
    def _():
        for field in range(2):
            halo(field, 0).wait_send()

    others.wait_send()


def local(tiles, depths, dissolved, sorbed, table):
    depth, rows, columns = dissolved.shape
    group = tiles * depths
    assert rows == group and rows % ROWS == 0 and columns % LANES == 0 and depth >= REACH
    shift = 0 if rows == ROWS else ROWS
    halves = columns // LANES
    padded = depth + 2 * REACH
    return pl.pallas_call(
        functools.partial(kernel, tiles, depths),
        out_shape=(
            jax.ShapeDtypeStruct((2, depth, rows, columns), jnp.float32),
            jax.ShapeDtypeStruct((4, rows // group, columns), jnp.float32),
        ),
        in_specs=[pl.BlockSpec(memory_space=pltpu.VMEM)] * 3,
        out_specs=(pl.BlockSpec(memory_space=pltpu.VMEM),) * 2,
        scratch_shapes=[
            pltpu.VMEM((2, padded, rows + 2 * shift, columns), jnp.bfloat16),
            pltpu.VMEM((6 * depth * ROWS, padded * (ROWS + 2 * shift)), jnp.bfloat16),
            pltpu.VMEM((4, columns, columns), jnp.bfloat16),
            pltpu.VMEM((4, depth, ROWS, columns), jnp.float32),
            pltpu.VMEM((group, 4 * halves, LANES), jnp.float32),
            pltpu.VMEM((group, 4 * halves, LANES), jnp.float32),
            pltpu.SemaphoreType.DMA((4,)),
            pltpu.SemaphoreType.DMA((4,)),
            pltpu.SemaphoreType.DMA,
            pltpu.SemaphoreType.DMA,
        ],
        compiler_params=pltpu.CompilerParams(
            collective_id=0, has_side_effects=True, vmem_limit_bytes=32 * 1024 * 1024
        ),
    )(dissolved, sorbed, table)


def solution(mesh):
    return jax.shard_map(
        functools.partial(local, mesh.shape["tile"], mesh.shape["depth"]),
        mesh=mesh,
        in_specs=(
            P(("run", "tile", "depth"), None, None),
            P(("run", "tile", "depth"), None, None),
            P(),
        ),
        out_specs=(
            P(None, ("run", "tile", "depth"), None, None),
            P(None, ("run", "tile", "depth"), None),
        ),
        check_vma=False,
    )
```

time: 151 us -> 16.8 us (0.11)
  local copies, waits for them, and re-layouts: 120 us -> 3.44 us
  starting transfers between devices: 13.3 us -> 0 us
  Pallas kernels: 0 us -> 12.4 us
  waiting for transfers between devices: 9.63 us -> 0 us
  other arithmetic: 3.18 us -> 0 us
  matrix products: 2.85 us -> 0 us
    gather x4 -> x0, local copies, waits for them, and re-layouts: 119 us -> none  [the longest x2 59.7 us: shade_cells(): lower_entry = jnp.take(table, index_low, axis=1)]
    ppermute x6 -> x0, starting transfers between devices: 13.3 us -> none  [the longest x4 9.65 us: swapped(): return lax.ppermute(block, axis, route)]
    pallas_call x0 -> x1, Pallas kernels: none -> 12.4 us  [local(): pl.pallas_call(functools.partial(kernel, tiles, depths), out_shape=(jax.S...]
    ppermute x6 -> x0, waiting for transfers between devices: 9.63 us -> none  [the longest x4 6.56 us: swapped(): return lax.ppermute(block, axis, route)]
    dot_general x6 -> x0, matrix products: 2.85 us -> none  [the longest x3 2.03 us: filter_columns(): jnp.einsum('fzxy,wy->fzxw', source, matrix, precision=lax.Precision.HIGHEST)]
    unnamed x6 -> x8, local copies, waits for them, and re-layouts: 0.89 us -> 3.44 us
  transfers between devices with their start and end apart: 6 -> 0, of which waited for: 5 -> 0; matrix products, arithmetic and copies ran while one was open for 1% -> 0% of each run, Pallas kernels for 0% -> 0%
where the time goes in v1:
time: 16.8 us; the launch traced here: 16.5 us
  Pallas kernels  12.4 us (74%)
  local copies, waits for them, and re-layouts  3.44 us (20%)
  between operations  0.65 us (4%)
    pallas_call x1, Pallas kernels, local(): pl.pallas_call(functools.partial(kernel, tiles, depths), out_shape=(jax.S...  12.4 us
    unnamed x8, local copies, waits for them, and re-layouts  3.44 us

profile of v1, /device:TPU:0, one launch (start us, length us, event | category | flops | bytes accessed | tf_op | source)
XLA Modules:
  0.0 16.5 jit_solution(8051107504989818206)
XLA Ops:
  0.6 0.0 copy-start
  0.6 0.7 %copy-done = bf16[4,16,256]{2,1,0:T(8,128)(2,1)S(1)} copy-done((bf16[4,16,256]{2,1,0:T(8,128)(2,1)S(1)}, bf16[4,16,256]{2,1,0:T(8,128)(2,1)}, u32[]{:S(2)}) %copy-start) | copy-done | bytes 32792
  1.4 0.0 copy-start.1
  1.4 0.8 %copy-done.1 = bf16[4,16,256]{2,1,0:T(8,128)(2,1)S(1)} copy-done((bf16[4,16,256]{2,1,0:T(8,128)(2,1)S(1)}, bf16[4,16,256]{2,1,0:T(8,128)(2,1)}, u32[]{:S(2)}) %copy-start.1) | copy-done | bytes 32792
  2.1 0.0 copy-start.2
  2.1 0.7 %copy-done.2 = f32[4,256]{1,0:T(4,128)S(1)} copy-done((f32[4,256]{1,0:T(4,128)S(1)}, f32[4,256]{1,0:T(4,128)}, u32[]{:S(2)}) %copy-start.2) | copy-done | bytes 4120
  2.8 12.4 %shard_map.50 = (f32[2,4,16,256]{3,2,1,0:T(8,128)S(1)}, f32[4,1,256]{2,1,0:T(1,128)S(1)}) custom-call(bf16[4,16,256]{2,1,0:T(8,128)(2,1)S(1)} %copy-done, bf16[4,16,256]{2,1,0:T(8,128)(2,1)S(1)} %copy-done.1, f32[4,256]{1,0:T(4,128)S(1)} %copy-done.2), custom_call_target="tpu_custom_call" | custom-call | tf_op jit(solution)/shard_map/pallas_call | solution.py:311
  15.2 0.7 %copy.7 = f32[2,4,16,256]{3,2,1,0:T(8,128)} copy(f32[2,4,16,256]{3,2,1,0:T(8,128)S(1)} %get-tuple-element.4) | data formatting | bytes 262144
  15.9 0.6 %copy.8 = f32[4,1,256]{2,1,0:T(1,128)} copy(f32[4,1,256]{2,1,0:T(1,128)S(1)} %get-tuple-element.5) | data formatting | bytes 8192
Async XLA Ops:
  0.6 0.8 %copy-start = (bf16[4,16,256]{2,1,0:T(8,128)(2,1)S(1)}, bf16[4,16,256]{2,1,0:T(8,128)(2,1)}, u32[]{:S(2)}) copy-start(bf16[4,16,256]{2,1,0:T(8,128)(2,1)} %dissolved.1) | copy-start | bytes 98308
  1.4 0.8 %copy-start.1 = (bf16[4,16,256]{2,1,0:T(8,128)(2,1)S(1)}, bf16[4,16,256]{2,1,0:T(8,128)(2,1)}, u32[]{:S(2)}) copy-start(bf16[4,16,256]{2,1,0:T(8,128)(2,1)} %sorbed.1) | copy-start | bytes 98308
  2.1 0.7 %copy-start.2 = (f32[4,256]{1,0:T(4,128)S(1)}, f32[4,256]{1,0:T(4,128)}, u32[]{:S(2)}) copy-start(f32[4,256]{1,0:T(4,128)} %table_ref.1) | copy-start | bytes 12292

commit v2 on v1

--- a/solution.py
+++ b/solution.py
@@ -89,9 +89,9 @@
 
 
 def kernel(
-    tiles, depths, dissolved, sorbed, table_ref, norms, rendered,
-    cells, weights, lines, looked, send, recv,
-    halo_send, halo_recv, image_send, image_recv,
+    tiles, depths, dissolved, sorbed, table_in, norms, recv,
+    cells, table_ref, weights, lines, looked, send,
+    load_sem, halo_send, halo_recv, image_send, image_recv,
 ):
     depth, rows, columns = dissolved.shape
     group = tiles * depths
@@ -102,6 +102,7 @@
     halves = columns // LANES
     run = lax.axis_index("run")
     me = lax.axis_index("tile") * depths + lax.axis_index("depth")
+    inner = pl.ds(shift, rows)
 
     def device(slab):
         return (run, slab // depths, slab % depths)
@@ -117,9 +118,38 @@
 
     barrier = pltpu.get_barrier_semaphore()
     peers(lambda p: pl.semaphore_signal(barrier, inc=1, device_id=device(p), device_id_type=MESH))
+
+    loads = [
+        pltpu.make_async_copy(dissolved, cells.at[0, pl.ds(REACH, depth), inner], load_sem.at[0]),
+        pltpu.make_async_copy(table_in, table_ref, load_sem.at[1]),
+        pltpu.make_async_copy(sorbed, cells.at[1, pl.ds(REACH, depth), inner], load_sem.at[2]),
+    ]
+    for load in loads:
+        load.start()
+
+    first, last = me == 0, me == group - 1
+
+    @pl.when(first)
+    def _():
+        for field in range(2):
+            cells[field, pl.ds(0, REACH), inner] = jnp.zeros((REACH, rows, columns), jnp.bfloat16)
+
+    @pl.when(last)
+    def _():
+        for field in range(2):
+            cells[field, pl.ds(depth + REACH, REACH), inner] = jnp.zeros(
+                (REACH, rows, columns), jnp.bfloat16
+            )
+
+    if shift:
+        edge = jnp.zeros((depth + 2 * REACH, shift, columns), jnp.bfloat16)
+        for field in range(2):
+            cells[field, :, pl.ds(0, shift)] = edge
+            cells[field, :, pl.ds(shift + rows, shift)] = edge
+
+    plane_weights(weights, depth, window, shift)
+
     pl.semaphore_wait(barrier, group - 1)
-
-    inner = pl.ds(shift, rows)
 
     def halo(field, up):
         source = (dissolved, sorbed)[field]
@@ -133,8 +163,6 @@
             device_id_type=MESH,
         )
 
-    first, last = me == 0, me == group - 1
-
     @pl.when(jnp.logical_not(last))
     def _():
         for field in range(2):
@@ -145,35 +173,16 @@
         for field in range(2):
             halo(field, 0).start()
 
-    @pl.when(first)
-    def _():
-        for field in range(2):
-            cells[field, pl.ds(0, REACH), inner] = jnp.zeros((REACH, rows, columns), jnp.bfloat16)
-
-    @pl.when(last)
-    def _():
-        for field in range(2):
-            cells[field, pl.ds(depth + REACH, REACH), inner] = jnp.zeros(
-                (REACH, rows, columns), jnp.bfloat16
-            )
-
-    if shift:
-        edge = jnp.zeros((depth + 2 * REACH, shift, columns), jnp.bfloat16)
-        for field in range(2):
-            cells[field, :, pl.ds(0, shift)] = edge
-            cells[field, :, pl.ds(shift + rows, shift)] = edge
-    cells[0, pl.ds(REACH, depth), inner] = dissolved[...]
-    cells[1, pl.ds(REACH, depth), inner] = sorbed[...]
-
-    plane_weights(weights, depth, window, shift)
     line_weights(lines, columns)
+    for load in loads:
+        load.wait()
 
     table = table_ref[...]
     step = pltpu.roll(table, table.shape[1] - 1, 1) - table
 
     def look(x0):
         for z in range(depth):
-            level = dissolved[z, pl.ds(x0, ROWS), :].astype(jnp.float32)
+            level = cells[0, REACH + z, pl.ds(shift + x0, ROWS), :].astype(jnp.float32)
             position = (table.shape[1] - 1.0) / (1.0 + jnp.exp(-level))
             for h in range(halves):
                 span = slice(h * LANES, (h + 1) * LANES)
@@ -263,6 +272,16 @@
     peers(lambda p: image(p).start())
     recv[me] = send[me]
 
+    @pl.when(jnp.logical_not(last))
+    def _():
+        for field in range(2):
+            halo(field, 1).wait_send()
+
+    @pl.when(jnp.logical_not(first))
+    def _():
+        for field in range(2):
+            halo(field, 0).wait_send()
+
     others = pltpu.make_async_remote_copy(
         src_ref=send.at[pl.ds(0, group - 1)],
         dst_ref=recv.at[pl.ds(0, group - 1)],
@@ -271,12 +290,19 @@
         device_id=device(lax.rem(me + 1, group)),
         device_id_type=MESH,
     )
+    others.wait_send()
     others.wait_recv()
 
+
+def finish(norms_in, pieces, norms_out, rendered_out, rendered, sem):
+    group, parts, _ = pieces.shape
+    halves = parts // 4
+    norms_copy = pltpu.make_async_copy(norms_in, norms_out, sem.at[0])
+    norms_copy.start()
     order = lax.broadcasted_iota(jnp.int32, (group, LANES), 0)
     for h in range(halves):
         span = slice(h * LANES, (h + 1) * LANES)
-        through = recv[:, 3 * halves + h, :]
+        through = pieces[:, 3 * halves + h, :]
         hop = 1
         while hop < group:
             through = through * jnp.where(order >= hop, pltpu.roll(through, hop, 0), 1.0)
@@ -284,21 +310,13 @@
         ahead = jnp.where(order >= 1, pltpu.roll(through, 1, 0), 1.0)
         for c in range(3):
             rendered[c, :, span] = jnp.sum(
-                recv[:, c * halves + h, :] * ahead, axis=0, keepdims=True
+                pieces[:, c * halves + h, :] * ahead, axis=0, keepdims=True
             )
         rendered[3, :, span] = 1.0 - through[group - 1 :]
-
-    @pl.when(jnp.logical_not(last))
-    def _():
-        for field in range(2):
-            halo(field, 1).wait_send()
-
-    @pl.when(jnp.logical_not(first))
-    def _():
-        for field in range(2):
-            halo(field, 0).wait_send()
-
-    others.wait_send()
+    rendered_copy = pltpu.make_async_copy(rendered, rendered_out, sem.at[1])
+    rendered_copy.start()
+    norms_copy.wait()
+    rendered_copy.wait()
 
 
 def local(tiles, depths, dissolved, sorbed, table):
@@ -308,21 +326,22 @@
     shift = 0 if rows == ROWS else ROWS
     halves = columns // LANES
     padded = depth + 2 * REACH
-    return pl.pallas_call(
+    norms, pieces = pl.pallas_call(
         functools.partial(kernel, tiles, depths),
         out_shape=(
             jax.ShapeDtypeStruct((2, depth, rows, columns), jnp.float32),
-            jax.ShapeDtypeStruct((4, rows // group, columns), jnp.float32),
-        ),
-        in_specs=[pl.BlockSpec(memory_space=pltpu.VMEM)] * 3,
+            jax.ShapeDtypeStruct((group, 4 * halves, LANES), jnp.float32),
+        ),
+        in_specs=[pl.BlockSpec(memory_space=pltpu.HBM)] * 3,
         out_specs=(pl.BlockSpec(memory_space=pltpu.VMEM),) * 2,
         scratch_shapes=[
             pltpu.VMEM((2, padded, rows + 2 * shift, columns), jnp.bfloat16),
+            pltpu.VMEM(table.shape, jnp.float32),
             pltpu.VMEM((6 * depth * ROWS, padded * (ROWS + 2 * shift)), jnp.bfloat16),
             pltpu.VMEM((4, columns, columns), jnp.bfloat16),
             pltpu.VMEM((4, depth, ROWS, columns), jnp.float32),
             pltpu.VMEM((group, 4 * halves, LANES), jnp.float32),
-            pltpu.VMEM((group, 4 * halves, LANES), jnp.float32),
+            pltpu.SemaphoreType.DMA((3,)),
             pltpu.SemaphoreType.DMA((4,)),
             pltpu.SemaphoreType.DMA((4,)),
             pltpu.SemaphoreType.DMA,
@@ -332,6 +351,20 @@
             collective_id=0, has_side_effects=True, vmem_limit_bytes=32 * 1024 * 1024
         ),
     )(dissolved, sorbed, table)
+    return pl.pallas_call(
+        finish,
+        out_shape=(
+            jax.ShapeDtypeStruct((2, depth, rows, columns), jnp.float32),
+            jax.ShapeDtypeStruct((4, rows // group, columns), jnp.float32),
+        ),
+        in_specs=[pl.BlockSpec(memory_space=pltpu.VMEM)] * 2,
+        out_specs=(pl.BlockSpec(memory_space=pltpu.HBM),) * 2,
+        scratch_shapes=[
+            pltpu.VMEM((4, rows // group, columns), jnp.float32),
+            pltpu.SemaphoreType.DMA((2,)),
+        ],
+        compiler_params=pltpu.CompilerParams(vmem_limit_bytes=16 * 1024 * 1024),
+    )(norms, pieces)
 
 
 def solution(mesh):

time: 16.8 us -> 16.2 us (0.964)
  local copies, waits for them, and re-layouts: 3.44 us -> 2.19 us
  Pallas kernels: 12.4 us -> 13.1 us
    unnamed x8 -> x6, local copies, waits for them, and re-layouts: 3.44 us -> 2.19 us
    pallas_call x0 -> x1, Pallas kernels: none -> 0.68 us  [local(): pl.pallas_call(finish, out_shape=(jax.ShapeDtypeStruct((2, depth, rows, c...]
where the time goes in v2:
time: 16.2 us; the launch traced here: 15.9 us
  Pallas kernels  13.1 us (81%)
  local copies, waits for them, and re-layouts  2.19 us (14%)
  between operations  0.65 us (4%)
    pallas_call x1, Pallas kernels, local(): pl.pallas_call(functools.partial(kernel, tiles, depths), out_shape=(jax.S...  12.4 us
    unnamed x6, local copies, waits for them, and re-layouts  2.19 us
    pallas_call x1, Pallas kernels, local(): pl.pallas_call(finish, out_shape=(jax.ShapeDtypeStruct((2, depth, rows, c...  0.68 us

profile of v2, /device:TPU:0, one launch (start us, length us, event | category | flops | bytes accessed | tf_op | source)
XLA Modules:
  0.0 15.9 jit_solution(6882985984759931551)
XLA Ops:
  0.6 0.0 copy-start
  0.6 0.7 %copy-done = bf16[4,16,256]{2,1,0:T(8,128)(2,1)S(1)} copy-done((bf16[4,16,256]{2,1,0:T(8,128)(2,1)S(1)}, bf16[4,16,256]{2,1,0:T(8,128)(2,1)}, u32[]{:S(2)}) %copy-start) | copy-done | bytes 32792
  1.4 0.0 copy-start.1
  1.4 0.8 %copy-done.1 = bf16[4,16,256]{2,1,0:T(8,128)(2,1)S(1)} copy-done((bf16[4,16,256]{2,1,0:T(8,128)(2,1)S(1)}, bf16[4,16,256]{2,1,0:T(8,128)(2,1)}, u32[]{:S(2)}) %copy-start.1) | copy-done | bytes 32792
  2.1 0.0 copy-start.2
  2.1 0.7 %copy-done.2 = f32[4,256]{1,0:T(4,128)S(1)} copy-done((f32[4,256]{1,0:T(4,128)S(1)}, f32[4,256]{1,0:T(4,128)}, u32[]{:S(2)}) %copy-start.2) | copy-done | bytes 4120
  2.8 12.4 %shard_map.50 = (f32[2,4,16,256]{3,2,1,0:T(8,128)S(1)}, f32[16,8,128]{2,1,0:T(8,128)S(1)}) custom-call(bf16[4,16,256]{2,1,0:T(8,128)(2,1)S(1)} %copy-done, bf16[4,16,256]{2,1,0:T(8,128)(2,1)S(1)} %copy-done.1, f32[4,256]{1,0:T(4,128)S(1)} %copy-done.2), custom_call_target="tpu_custom_call" | custom-call | tf_op jit(solution)/shard_map/pallas_call | solution.py:329
  15.2 0.7 %shard_map.51 = (f32[2,4,16,256]{3,2,1,0:T(8,128)}, f32[4,1,256]{2,1,0:T(1,128)}) custom-call(f32[2,4,16,256]{3,2,1,0:T(8,128)S(1)} %get-tuple-element.4.norms_in, f32[16,8,128]{2,1,0:T(8,128)S(1)} %get-tuple-element.5.pieces), custom_call_target="tpu_custom_call" | custom-call | tf_op jit(solution)/shard_map/pallas_call | solution.py:354
Async XLA Ops:
  0.6 0.8 %copy-start = (bf16[4,16,256]{2,1,0:T(8,128)(2,1)S(1)}, bf16[4,16,256]{2,1,0:T(8,128)(2,1)}, u32[]{:S(2)}) copy-start(bf16[4,16,256]{2,1,0:T(8,128)(2,1)} %dissolved.1) | copy-start | bytes 98308
  1.4 0.8 %copy-start.1 = (bf16[4,16,256]{2,1,0:T(8,128)(2,1)S(1)}, bf16[4,16,256]{2,1,0:T(8,128)(2,1)}, u32[]{:S(2)}) copy-start(bf16[4,16,256]{2,1,0:T(8,128)(2,1)} %sorbed.1) | copy-start | bytes 98308
  2.1 0.7 %copy-start.2 = (f32[4,256]{1,0:T(4,128)S(1)}, f32[4,256]{1,0:T(4,128)}, u32[]{:S(2)}) copy-start(f32[4,256]{1,0:T(4,128)} %table_in.1) | copy-start | bytes 12292

commit v3 on v2

--- a/solution.py
+++ b/solution.py
@@ -320,6 +320,9 @@
 
 
 def local(tiles, depths, dissolved, sorbed, table):
+    dissolved, sorbed, table = (
+        pltpu.with_memory_space_constraint(whole, pltpu.HBM) for whole in (dissolved, sorbed, table)
+    )
     depth, rows, columns = dissolved.shape
     group = tiles * depths
     assert rows == group and rows % ROWS == 0 and columns % LANES == 0 and depth >= REACH

time: 16.2 us -> 14.2 us (0.88)
  local copies, waits for them, and re-layouts: 2.19 us -> 0 us
  Pallas kernels: 13.1 us -> 13.4 us
    unnamed x6 -> x0, local copies, waits for them, and re-layouts: 2.19 us -> none
    pallas_call x1, Pallas kernels: 12.4 us -> 12.7 us  [local(): pl.pallas_call(functools.partial(kernel, tiles, depths), out_shape=(jax.S...]
where the time goes in v3:
time: 14.2 us; the launch traced here: 14 us
  Pallas kernels  13.4 us (94%)
  between operations  0.64 us (5%)
    pallas_call x1, Pallas kernels, local(): pl.pallas_call(functools.partial(kernel, tiles, depths), out_shape=(jax.S...  12.7 us
    pallas_call x1, Pallas kernels, local(): pl.pallas_call(finish, out_shape=(jax.ShapeDtypeStruct((2, depth, rows, c...  0.68 us

profile of v3, /device:TPU:0, one launch (start us, length us, event | category | flops | bytes accessed | tf_op | source)
XLA Modules:
  0.0 14.0 jit_solution(13909246996062238695)
XLA Ops:
  0.6 12.7 %shard_map.50 = (f32[2,4,16,256]{3,2,1,0:T(8,128)S(1)}, f32[16,8,128]{2,1,0:T(8,128)S(1)}) custom-call(bf16[4,16,256]{2,1,0:T(8,128)(2,1)} %dissolved.1, bf16[4,16,256]{2,1,0:T(8,128)(2,1)} %sorbed.1, f32[4,256]{1,0:T(4,128)} %table_in.1), custom_call_target="tpu_custom_call" | custom-call | tf_op jit(solution)/shard_map/pallas_call | solution.py:332
  13.4 0.7 %shard_map.51 = (f32[2,4,16,256]{3,2,1,0:T(8,128)}, f32[4,1,256]{2,1,0:T(1,128)}) custom-call(f32[2,4,16,256]{3,2,1,0:T(8,128)S(1)} %get-tuple-element.4.norms_in, f32[16,8,128]{2,1,0:T(8,128)S(1)} %get-tuple-element.5.pieces), custom_call_target="tpu_custom_call" | custom-call | tf_op jit(solution)/shard_map/pallas_call | solution.py:357

commit v4 on v3

--- a/solution.py
+++ b/solution.py
@@ -91,7 +91,7 @@
 def kernel(
     tiles, depths, dissolved, sorbed, table_in, norms, recv,
     cells, table_ref, weights, lines, looked, send,
-    load_sem, halo_send, halo_recv, image_send, image_recv,
+    load_sem, halo_send, halo_recv, image_send, image_recv, ready,
 ):
     depth, rows, columns = dissolved.shape
     group = tiles * depths
@@ -107,17 +107,19 @@
     def device(slab):
         return (run, slab // depths, slab % depths)
 
-    def peers(body):
-        if group <= 32:
-            for k in range(1, group):
-                body(lax.rem(me + k, group))
-        else:
-            @pl.loop(1, group)
-            def _(k):
-                body(lax.rem(me + k, group))
+    def each(start, stop, body):
+        lax.fori_loop(start, stop, lambda slab, carry: (body(slab), carry)[1], 0)
 
     barrier = pltpu.get_barrier_semaphore()
-    peers(lambda p: pl.semaphore_signal(barrier, inc=1, device_id=device(p), device_id_type=MESH))
+
+    def greet(slab):
+        pl.semaphore_signal(barrier, inc=1, device_id=device(slab), device_id_type=MESH)
+
+    def call_ready(slab):
+        pl.semaphore_signal(ready, inc=1, device_id=device(slab), device_id_type=MESH)
+
+    each(jnp.maximum(me - 1, 0), me, greet)
+    each(me + 1, group, greet)
 
     loads = [
         pltpu.make_async_copy(dissolved, cells.at[0, pl.ds(REACH, depth), inner], load_sem.at[0]),
@@ -149,13 +151,14 @@
 
     plane_weights(weights, depth, window, shift)
 
-    pl.semaphore_wait(barrier, group - 1)
+    for load in loads:
+        load.wait()
+    pl.semaphore_wait(barrier, jnp.minimum(me + 1, group - 1))
 
     def halo(field, up):
-        source = (dissolved, sorbed)[field]
         k = 2 * field + up
         return pltpu.make_async_remote_copy(
-            src_ref=source.at[pl.ds(depth - REACH, REACH)] if up else source.at[pl.ds(0, REACH)],
+            src_ref=cells.at[field, pl.ds(depth if up else REACH, REACH), inner],
             dst_ref=cells.at[field, pl.ds(0 if up else depth + REACH, REACH), inner],
             send_sem=halo_send.at[k],
             recv_sem=halo_recv.at[k],
@@ -173,9 +176,8 @@
         for field in range(2):
             halo(field, 0).start()
 
+    each(0, me - 1, call_ready)
     line_weights(lines, columns)
-    for load in loads:
-        load.wait()
 
     table = table_ref[...]
     step = pltpu.roll(table, table.shape[1] - 1, 1) - table
@@ -269,7 +271,14 @@
             device_id_type=MESH,
         )
 
-    peers(lambda p: image(p).start())
+    each(0, me, lambda slab: image(slab).start())
+    each(me + 1, jnp.minimum(me + 2, group), lambda slab: image(slab).start())
+
+    @pl.when(me < group - 2)
+    def _():
+        pl.semaphore_wait(ready, group - 2 - me)
+
+    each(me + 2, group, lambda slab: image(slab).start())
     recv[me] = send[me]
 
     @pl.when(jnp.logical_not(last))
@@ -349,6 +358,7 @@
             pltpu.SemaphoreType.DMA((4,)),
             pltpu.SemaphoreType.DMA,
             pltpu.SemaphoreType.DMA,
+            pltpu.SemaphoreType.REGULAR,
         ],
         compiler_params=pltpu.CompilerParams(
             collective_id=0, has_side_effects=True, vmem_limit_bytes=32 * 1024 * 1024

time: 14.2 us -> 13.5 us (0.951)
  Pallas kernels: 13.4 us -> 12.7 us
    pallas_call x1, Pallas kernels: 12.7 us -> 12 us  [local(): pl.pallas_call(functools.partial(kernel, tiles, depths), out_shape=(jax.S...]
where the time goes in v4:
time: 13.5 us; the launch traced here: 13.3 us
  Pallas kernels  12.7 us (94%)
  between operations  0.64 us (5%)
    pallas_call x1, Pallas kernels, local(): pl.pallas_call(functools.partial(kernel, tiles, depths), out_shape=(jax.S...  12 us
    pallas_call x1, Pallas kernels, local(): pl.pallas_call(finish, out_shape=(jax.ShapeDtypeStruct((2, depth, rows, c...  0.68 us

profile of v4, /device:TPU:0, one launch (start us, length us, event | category | flops | bytes accessed | tf_op | source)
XLA Modules:
  0.0 13.3 jit_solution(10601251773717134166)
XLA Ops:
  0.6 12.0 %shard_map.50 = (f32[2,4,16,256]{3,2,1,0:T(8,128)S(1)}, f32[16,8,128]{2,1,0:T(8,128)S(1)}) custom-call(bf16[4,16,256]{2,1,0:T(8,128)(2,1)} %dissolved.1, bf16[4,16,256]{2,1,0:T(8,128)(2,1)} %sorbed.1, f32[4,256]{1,0:T(4,128)} %table_in.1), custom_call_target="tpu_custom_call" | custom-call | tf_op jit(solution)/shard_map/pallas_call | solution.py:341
  12.6 0.7 %shard_map.51 = (f32[2,4,16,256]{3,2,1,0:T(8,128)}, f32[4,1,256]{2,1,0:T(1,128)}) custom-call(f32[2,4,16,256]{3,2,1,0:T(8,128)S(1)} %get-tuple-element.4.norms_in, f32[16,8,128]{2,1,0:T(8,128)S(1)} %get-tuple-element.5.pieces), custom_call_target="tpu_custom_call" | custom-call | tf_op jit(solution)/shard_map/pallas_call | solution.py:367

commit v5 on v4

--- a/solution.py
+++ b/solution.py
@@ -155,26 +155,23 @@
         load.wait()
     pl.semaphore_wait(barrier, jnp.minimum(me + 1, group - 1))
 
-    def halo(field, up):
-        k = 2 * field + up
+    def halo(up):
         return pltpu.make_async_remote_copy(
-            src_ref=cells.at[field, pl.ds(depth if up else REACH, REACH), inner],
-            dst_ref=cells.at[field, pl.ds(0 if up else depth + REACH, REACH), inner],
-            send_sem=halo_send.at[k],
-            recv_sem=halo_recv.at[k],
+            src_ref=cells.at[:, pl.ds(depth if up else REACH, REACH), inner],
+            dst_ref=cells.at[:, pl.ds(0 if up else depth + REACH, REACH), inner],
+            send_sem=halo_send.at[up],
+            recv_sem=halo_recv.at[up],
             device_id=device(me + 1 if up else me - 1),
             device_id_type=MESH,
         )
 
     @pl.when(jnp.logical_not(last))
     def _():
-        for field in range(2):
-            halo(field, 1).start()
+        halo(1).start()
 
     @pl.when(jnp.logical_not(first))
     def _():
-        for field in range(2):
-            halo(field, 0).start()
+        halo(0).start()
 
     each(0, me - 1, call_ready)
     line_weights(lines, columns)
@@ -240,13 +237,11 @@
     def arrive():
         @pl.when(jnp.logical_not(first))
         def _():
-            for field in range(2):
-                halo(field, 1).wait_recv()
+            halo(1).wait_recv()
 
         @pl.when(jnp.logical_not(last))
         def _():
-            for field in range(2):
-                halo(field, 0).wait_recv()
+            halo(0).wait_recv()
 
     if chunks == 1:
         look(0)
@@ -283,13 +278,11 @@
 
     @pl.when(jnp.logical_not(last))
     def _():
-        for field in range(2):
-            halo(field, 1).wait_send()
+        halo(1).wait_send()
 
     @pl.when(jnp.logical_not(first))
     def _():
-        for field in range(2):
-            halo(field, 0).wait_send()
+        halo(0).wait_send()
 
     others = pltpu.make_async_remote_copy(
         src_ref=send.at[pl.ds(0, group - 1)],
@@ -354,8 +347,8 @@
             pltpu.VMEM((4, depth, ROWS, columns), jnp.float32),
             pltpu.VMEM((group, 4 * halves, LANES), jnp.float32),
             pltpu.SemaphoreType.DMA((3,)),
-            pltpu.SemaphoreType.DMA((4,)),
-            pltpu.SemaphoreType.DMA((4,)),
+            pltpu.SemaphoreType.DMA((2,)),
+            pltpu.SemaphoreType.DMA((2,)),
             pltpu.SemaphoreType.DMA,
             pltpu.SemaphoreType.DMA,
             pltpu.SemaphoreType.REGULAR,

time: 13.5 us -> 13.5 us (level)
  no operation moved by 1% of the time
where the time goes in v5:
time: 13.5 us; the launch traced here: 13.3 us
  Pallas kernels  12.6 us (93%)
  between operations  0.64 us (5%)
    pallas_call x1, Pallas kernels, local(): pl.pallas_call(functools.partial(kernel, tiles, depths), out_shape=(jax.S...  12 us
    pallas_call x1, Pallas kernels, local(): pl.pallas_call(finish, out_shape=(jax.ShapeDtypeStruct((2, depth, rows, c...  0.68 us

profile of v5, /device:TPU:0, one launch (start us, length us, event | category | flops | bytes accessed | tf_op | source)
XLA Modules:
  0.0 13.3 jit_solution(11860515346009293599)
XLA Ops:
  0.6 12.0 %shard_map.50 = (f32[2,4,16,256]{3,2,1,0:T(8,128)S(1)}, f32[16,8,128]{2,1,0:T(8,128)S(1)}) custom-call(bf16[4,16,256]{2,1,0:T(8,128)(2,1)} %dissolved.1, bf16[4,16,256]{2,1,0:T(8,128)(2,1)} %sorbed.1, f32[4,256]{1,0:T(4,128)} %table_in.1), custom_call_target="tpu_custom_call" | custom-call | tf_op jit(solution)/shard_map/pallas_call | solution.py:334
  12.6 0.7 %shard_map.51 = (f32[2,4,16,256]{3,2,1,0:T(8,128)}, f32[4,1,256]{2,1,0:T(1,128)}) custom-call(f32[2,4,16,256]{3,2,1,0:T(8,128)S(1)} %get-tuple-element.4.norms_in, f32[16,8,128]{2,1,0:T(8,128)S(1)} %get-tuple-element.5.pieces), custom_call_target="tpu_custom_call" | custom-call | tf_op jit(solution)/shard_map/pallas_call | solution.py:360
